TPU v7x, 512 devices: a whole 4x4x16 slice. The times are simulated.
512 devices in a mesh: dp: 16 (over z), ctx: 32 (over x, y, core).
Axes of the slice: x: 4, y: 4, z: 16, core: 2. Of those that a mesh axis runs over, the one named last changes fastest.
Arguments:
- queries: bfloat16 [16, 4096, 2048], P('dp', 'ctx'), may hold values from -6 to 6
- keys: bfloat16 [16, 4096, 2048], P('dp', 'ctx'), may hold values from -6 to 6
- values: bfloat16 [16, 4096, 2048], P('dp', 'ctx'), may hold values from -6 to 6
- out_grad: bfloat16 [16, 4096, 2048], P('dp', 'ctx'), may hold values from -6 to 6
- map_weight: bfloat16 [16, 128, 128], replicated, may hold values from -0.5 to 0.5
Outputs:
- query_grad: bfloat16 [16, 4096, 2048], P('dp', 'ctx')
- key_grad: bfloat16 [16, 4096, 2048], P('dp', 'ctx')
- value_grad: bfloat16 [16, 4096, 2048], P('dp', 'ctx')
- map_grad: float32 [16, 128, 128], replicated
All inputs are finite; a program needn't handle non-finite values.
Results may differ from a plain program's by a relative error of at most 0.0096.
Values sent between devices are 32-bit elements; how exact they have to be, the bound alone decides.
A program may use at most 128 MiB of HBM per device.

v0:
```python
import jax
import jax.numpy as jnp
from jax import lax
from jax.sharding import PartitionSpec as P

HIGH = lax.Precision.HIGHEST


def prefix(part, axis, combine, identity, reverse):
    count = lax.axis_size(axis)
    place = lax.axis_index(axis)
    ahead = count - 1 - place if reverse else place
    gathered = jax.tree.map(lambda a: lax.all_gather(a, axis), part)
    state = jax.tree.map(lambda a, e: jnp.zeros_like(a) + jnp.asarray(e, a.dtype), part, identity)

    def one(hop, state):
        source = count - 1 - hop if reverse else hop
        return combine(
            state, jax.tree.map(lambda a: lax.dynamic_index_in_dim(a, source, 0, False), gathered)
        )

    return lax.fori_loop(0, ahead, one, state)


def add_pair(earlier, later):
    return (earlier[0] + later[0], earlier[1] + later[1])


def lowmult(form, left, right):
    return jnp.einsum(form, left, right, preferred_element_type=jnp.float32)


def fullmult(form, left, right):
    return jnp.einsum(form, left.astype(jnp.float32), right.astype(jnp.float32), precision=HIGH)


def per_device(queries, keys, values, out_grad, map_weight):
    heads = map_weight.shape[0]
    width = map_weight.shape[1]
    rows = queries.shape[1]

    def split(x):
        return x[0].reshape(rows, heads, width)

    query = split(queries)
    key_in = split(keys)
    value = split(values)
    grad_out = split(out_grad).astype(jnp.float32)
    q_pre = lowmult("the,hef->thf", query, map_weight)
    k_pre = lowmult("the,hef->thf", key_in, map_weight)
    q_feat = jax.nn.elu(q_pre) + 1.0
    k_feat = jax.nn.elu(k_pre) + 1.0
    q_low = q_feat.astype(jnp.bfloat16)
    k_low = k_feat.astype(jnp.bfloat16)
    state_own = lowmult("shi,shj->hij", k_low, value)
    keysum_own = jnp.sum(k_low.astype(jnp.float32), axis=0)
    zero_state = jnp.zeros_like(state_own)
    zero_sum = jnp.zeros_like(keysum_own)
    state_prev, keysum_prev = prefix(
        (state_own, keysum_own), "ctx", add_pair, (zero_state, zero_sum), False
    )
    state_low = state_prev.astype(jnp.bfloat16)
    place = jnp.arange(rows)
    causal = (place[:, None] >= place[None, :]).astype(jnp.float32)
    scores = lowmult("thi,shi->hts", q_low, k_low) * causal
    score_low = scores.astype(jnp.bfloat16)
    numer = lowmult("hts,she->the", score_low, value) + lowmult("thi,hij->thj", q_low, state_low)
    denom = jnp.sum(scores, axis=2).T + fullmult("thi,hi->th", q_low, keysum_prev)
    attended = numer / denom[:, :, None]
    scaled = (grad_out / denom[:, :, None]).astype(jnp.bfloat16)
    weight_den = -jnp.sum(grad_out * attended, axis=2) / denom
    grad_state_own = lowmult("thi,thj->hij", q_low, scaled)
    grad_sum_own = fullmult("th,thi->hi", weight_den, q_low)
    later_state, later_sum = prefix(
        (grad_state_own, grad_sum_own), "ctx", add_pair, (zero_state, zero_sum), True
    )
    later_low = later_state.astype(jnp.bfloat16)
    mixed = ((lowmult("the,she->hts", scaled, value) + weight_den.T[:, :, None]) * causal).astype(
        jnp.bfloat16
    )
    qf_grad = (
        lowmult("hts,shi->thi", mixed, k_low)
        + lowmult("the,hie->thi", scaled, state_low)
        + weight_den[:, :, None] * keysum_prev[None]
    )
    kf_grad = (
        lowmult("hts,thi->shi", mixed, q_low)
        + lowmult("shj,hij->shi", value, later_low)
        + later_sum[None]
    )
    v_grad = lowmult("hts,the->she", score_low, scaled) + lowmult("shi,hie->she", k_low, later_low)
    q_pre_grad = (qf_grad * jnp.where(q_pre > 0, 1.0, q_feat)).astype(jnp.bfloat16)
    k_pre_grad = (kf_grad * jnp.where(k_pre > 0, 1.0, k_feat)).astype(jnp.bfloat16)
    q_grad = lowmult("thf,hef->the", q_pre_grad, map_weight)
    k_grad = lowmult("thf,hef->the", k_pre_grad, map_weight)
    map_local = lowmult("the,thf->hef", query, q_pre_grad) + lowmult(
        "the,thf->hef", key_in, k_pre_grad
    )
    map_total = lax.psum(map_local, ("dp", "ctx"))

    def join(x):
        return x.reshape(1, rows, heads * width).astype(jnp.bfloat16)

    return (join(q_grad), join(k_grad), join(v_grad), map_total)


def solution(mesh):
    in_specs = (
        P("dp", "ctx", None),
        P("dp", "ctx", None),
        P("dp", "ctx", None),
        P("dp", "ctx", None),
        P(),
    )
    out_specs = (P("dp", "ctx", None), P("dp", "ctx", None), P("dp", "ctx", None), P())
    return jax.shard_map(
        per_device, mesh=mesh, in_specs=in_specs, out_specs=out_specs, check_vma=False
    )
```

profile of v0, /device:TPU:1, one launch (start us, length us, event | category | flops | bytes accessed | tf_op | source)
XLA Modules:
  0.0 854.0 jit_solution(14094391126823981700)
XLA Ops:
  9.8 1.5 convert_reduce_fusion
  12.7 2.2 copy.45
  16.2 28.6 %all-gather.1 = f32[512,128]{1,0:T(8,128)S(1)} all-gather(f32[16,128]{1,0:T(8,128)S(1)} %get-tuple-element.155), channel_id=3, replica_groups=mesh['dp'=16,'ctx'=32] {'ctx'}, dimensions={0}, use_global_device_ids=true | all-gather | bytes 270336 | tf_op jit(solution)/shard_map/all_gather | solution.py:13
  44.7 1.6 fusion.21
  47.6 100.2 %all-gather.7.cloned.1.call-done = f32[512,128,128]{2,1,0:T(8,128)} async-done(((f32[16,128,128]{2,1,0:T(8,128)}), f32[512,128,128]{2,1,0:T(8,128)}) %all-gather.7.cloned.1.call-update) | async-done | bytes 33554448 | tf_op jit(solution)/shard_map/all_gather | solution.py:13
  147.9 1.5 while.26
  147.9 1.5 bitcast_add_fusion.8
  153.8 1.9 fusion.15
  157.9 2.1 fusion.12
  162.9 68.2 %all-gather.3 = f32[512,128]{1,0:T(8,128)S(1)} all-gather(f32[16,128]{1,0:T(8,128)S(1)} %bitcast.138), channel_id=5, replica_groups=mesh['dp'=16,'ctx'=32] {'ctx'}, dimensions={0}, use_global_device_ids=true | all-gather | bytes 270336 | tf_op jit(solution)/shard_map/all_gather | solution.py:13
  231.1 2.5 fusion.37
  233.6 2.6 fusion.22
  236.2 91.4 %all-gather.9.cloned.1.call-done = f32[512,128,128]{2,1,0:T(8,128)} async-done(((f32[16,128,128]{2,1,0:T(8,128)}), f32[512,128,128]{2,1,0:T(8,128)}) %all-gather.9.cloned.1.call-update) | async-done | bytes 33554448 | tf_op jit(solution)/shard_map/all_gather | solution.py:13
  327.7 46.1 %while.27 = (s32[]{:T(128)}, f32[16,128,128]{2,1,0:T(8,128)S(1)}, f32[16,128]{1,0:T(8,128)S(1)}, s32[]{:T(128)}, f32[32,16,128,128]{3,2,1,0:T(8,128)}, /*index=5...) while((s32[]{:T(128)}, f32[16,128,128]{2,1,0:T(8,128)S(1)}, ...), condition=%wide.region_6.7_spmd, body=%wide.region_5.6_spmd.sunk | while | flops 264198 | bytes 3170467 | solution.py:22
  327.7 1.5 bitcast_add_fusion.10
  329.2 1.5 bitcast_add_fusion.10
  330.8 1.5 bitcast_add_fusion.10
  332.3 1.5 bitcast_add_fusion.10
  333.8 1.5 bitcast_add_fusion.10
  335.4 1.5 bitcast_add_fusion.10
  336.9 1.5 bitcast_add_fusion.10
  338.4 1.5 bitcast_add_fusion.10
  340.0 1.5 bitcast_add_fusion.10
  341.5 1.5 bitcast_add_fusion.10
  343.0 1.5 bitcast_add_fusion.10
  344.5 1.5 bitcast_add_fusion.10
  373.8 1.5 fusion.28
  375.3 2.1 fusion.14
  377.4 2.7 fusion.7
  381.7 1.7 fusion.13
  384.4 460.5 %all-reduce.2.cloned.1.call-done = f32[16,128,128]{1,2,0:T(8,128)} async-done(((f32[16,128,128]{1,2,0:T(8,128)}), f32[16,128,128]{1,2,0:T(8,128)}) %all-reduce.2.cloned.1.call-update) | async-done | bytes 1048592 | tf_op jit(solution)/shard_map/psum | solution.py:99
  844.9 2.5 copy.78
  (92 shorter events, 45.6 us)
Async XLA Ops:
  7.2 2.6 copy-start
  7.2 140.6 %all-gather.7.cloned.1.call-start = ((), (), s32[]{:S(2)}) async-start(), calls=%async_computation.1 | async-start | bytes 34603008 | tf_op jit(solution)/shard_map/all_gather | solution.py:13
  8.4 1.4 copy-start.3
  9.8 35.0 %copy-start.1 = (bf16[16,8,16,128]{3,2,1,0:T(8,128)(2,1)}, bf16[16,8,16,128]{3,2,1,0:T(8,128)(2,1)S(1)}, u32[]{:S(2)}) copy-start(bf16[16,8,16,128]{3,2,1,0:T(8,128)(2,1)S(1)} %copy.106) | copy-start | bytes 1572868
  12.7 314.9 %all-gather.9.cloned.1.call-start = ((), (), s32[]{:S(2)}) async-start(), calls=%async_computation.2 | async-start | bytes 34603008 | tf_op jit(solution)/shard_map/all_gather | solution.py:13
  16.1 131.7 %copy-start.4 = (bf16[16,8,16,128]{3,2,1,0:T(8,128)(2,1)}, bf16[16,8,16,128]{3,2,1,0:T(8,128)(2,1)S(1)}, u32[]{:S(2)}) copy-start(bf16[16,8,16,128]{3,2,1,0:T(8,128)(2,1)S(1)} %copy.107) | copy-start | bytes 1572868
  153.2 691.7 %all-reduce.2.cloned.1.call-start = ((), (), s32[]{:S(2)}) async-start(), calls=%async_computation | async-start | bytes 2097152 | tf_op jit(solution)/shard_map/psum | solution.py:99
  157.1 0.8 copy-start.5
  160.0 0.8 copy-start.2
Sparse Core Ops, SparseCore 0:
  12.8 134.9 all-gather.6
  153.4 174.1 all-gather.8
  380.3 464.6 all-reduce.1
where the time goes:
time: 856 us; the launch traced here: 854 us
  waiting for transfers between devices  652 us (76%)
  blocking collectives  96.8 us (11%)
  other arithmetic  47.9 us (6%)
  matrix products  29 us (3%)
  between operations  14 us (2%)
  local copies, waits for them, and re-layouts  13 us (2%)
    psum x1, waiting for transfers between devices, per_device(): map_total = lax.psum(map_local, ('dp', 'ctx'))  461 us
    all_gather x2, waiting for transfers between devices, prefix(): gathered = jax.tree.map(lambda a: lax.all_gather(a, axis), part)  192 us
    all_gather x2, blocking collectives, prefix(): gathered = jax.tree.map(lambda a: lax.all_gather(a, axis), part)  96.8 us
    add x62, other arithmetic, add_pair(): return (earlier[0] + later[0], earlier[1] + later[1])  46.5 us
    dot_general x18, matrix products, lowmult(): return jnp.einsum(form, left, right, preferred_element_type=jnp.float32)  27.6 us
  transfers between devices with their start and end apart: 3, of which 3 were waited for; matrix products, arithmetic and copies ran while one was open for 3% of the time, Pallas kernels for 0%

commit v1 on v0

v1 whole, which is shorter than its diff:
```python
import functools
import math

import jax
import jax.numpy as jnp
from jax import lax
from jax.experimental import pallas as pl
from jax.experimental.pallas import tpu as pltpu
from jax.sharding import PartitionSpec as P

GROUPS = 2
PAIR = 2
F32 = jnp.float32
BF16 = jnp.bfloat16


def nn(a, b):
    return lax.dot_general(a, b, (((1,), (0,)), ((), ())), preferred_element_type=F32)


def nt(a, b):
    return lax.dot_general(a, b, (((1,), (1,)), ((), ())), preferred_element_type=F32)


def tn(a, b):
    return lax.dot_general(a, b, (((0,), (0,)), ((), ())), preferred_element_type=F32)


class Sizes:
    def __init__(self, nz, nctx, heads, dim):
        self.nz = nz
        self.chips = nctx // 2
        self.ny = math.isqrt(self.chips)
        self.heads = heads
        self.half = heads // 2
        self.groups = GROUPS
        self.hc = self.half // GROUPS
        self.dim = dim
        self.rows = dim // self.chips


def scratch(s):
    d, hc, g, n = s.dim, s.hc, s.groups, s.chips
    dma = pltpu.SemaphoreType.DMA
    v = pltpu.VMEM
    return dict(
        qv=v((d, s.heads * d), BF16), kv=v((d, s.heads * d), BF16), vv=v((d, s.heads * d), BF16),
        gv=v((d, s.heads * d), BF16), wv=v((s.heads, d, d), BF16),
        qf=v((s.heads, d, d), BF16), kf=v((s.heads, d, d), BF16),
        dq=v((s.heads, d, d), F32), dk=v((s.heads, d, d), F32),
        sc=v((s.heads, d, d), BF16), scaled=v((s.heads, d, d), BF16),
        numer=v((s.heads, d, d), F32), denom=v((s.heads, d, 1), F32), wden=v((s.heads, d, 1), F32),
        kpart=v((s.heads, d, d), F32), vpart=v((s.heads, d, d), F32),
        own=v((3, s.heads, d, d), F32), ksown=v((2, 2, g, 8, d), F32),
        xr=v((3, s.half, d, d), F32), xk=v((2, g, 8, d), F32),
        comb=v((3, g, hc + 1, d, d), F32), recv=v((3, g, n, hc + 1, s.rows, d), F32),
        back=v((2, g, hc, d, d), F32), sib=v((2, g, hc, d, d), F32), ksib=v((2, g, 8, d), F32),
        state=v((2, s.heads, d, d), F32), kstate=v((2, 2, g, 8, d), F32),
        tsum=v((g, hc, s.rows, d), F32), zr=v((g, s.nz, s.rows, d), F32), fin=v((g, hc, s.rows, d), F32),
        qo=v((d, s.heads * d), BF16), ko=v((d, s.heads * d), BF16), vo=v((d, s.heads * d), BF16),
        mo=v((s.heads, d, d), F32),
        in_sem=dma((5,)), out_sem=dma((4,)),
        xs_sem=dma((3, s.half)), xr_sem=dma((3, s.half)), xks_sem=dma((2, g)), xkr_sem=dma((2, g)),
        as_sem=dma((3, g)), ar_sem=dma((3, g)),
        bs_sem=dma((3, g)), br_sem=dma((3, g, n)),
        ys_sem=dma((3, g)), yr_sem=dma((3, g)), yks_sem=dma((2, g)), ykr_sem=dma((2, g)),
        z1s_sem=dma((g,)), z1r_sem=dma((g,)), z2s_sem=dma((g,)), z2r_sem=dma((g,)),
    )


def kernel(s, names, q_hbm, k_hbm, v_hbm, g_hbm, w_hbm, qg_hbm, kg_hbm, vg_hbm, mg_hbm, *refs):
    r = dict(zip(names, refs))
    n, hc, d, half, rows = s.chips, s.hc, s.dim, s.half, s.rows
    z = lax.axis_index("dp")
    ctx = lax.axis_index("ctx")
    core = lax.rem(ctx, 2)
    chip = lax.div(ctx, 2)
    cx, cy = lax.div(chip, s.ny), lax.rem(chip, s.ny)
    coref = core.astype(F32)
    sibling = (z, chip * 2 + 1 - core)

    def peer(step):
        px = lax.rem(cx + lax.div(step, s.ny), s.ny)
        py = lax.rem(cy + lax.rem(step, s.ny), s.ny)
        return px * s.ny + py

    def source(step):
        px = lax.rem(cx + s.ny - lax.div(step, s.ny), s.ny)
        py = lax.rem(cy + s.ny - lax.rem(step, s.ny), s.ny)
        return px * s.ny + py

    def remote(src, dst, send, recv, device):
        return pltpu.make_async_remote_copy(
            src_ref=src, dst_ref=dst, send_sem=send, recv_sem=recv, device_id=device,
            device_id_type=pl.DeviceIdType.MESH)

    def wait_for(ref, sem):
        pltpu.make_async_copy(ref, ref, sem).wait()

    def rows_of(owner):
        return pl.ds(pl.multiple_of(owner * rows, rows), rows)

    def loop(lower, upper, body):
        def step(i, carry):
            body(i)
            return carry

        lax.fori_loop(lower, upper, step, 0)

    barrier = pltpu.get_barrier_semaphore()

    def greet(device):
        pl.semaphore_signal(barrier, inc=1, device_id=device, device_id_type=pl.DeviceIdType.MESH)

    greet(sibling)
    loop(1, n, lambda i: greet((z, peer(i) * 2 + core)))
    loop(1, s.nz, lambda i: greet((lax.rem(z + i, s.nz), ctx)))

    loads = [
        pltpu.make_async_copy(src, dst, r["in_sem"].at[i])
        for i, (src, dst) in enumerate((
            (w_hbm, r["wv"]), (k_hbm.at[0], r["kv"]), (v_hbm.at[0], r["vv"]), (q_hbm.at[0], r["qv"]),
            (g_hbm.at[0], r["gv"])))
    ]
    for load in loads:
        load.start()
    r["ksown"][...] = jnp.zeros_like(r["ksown"])
    for load in loads[:4]:
        load.wait()
    pl.semaphore_wait(barrier, n + s.nz - 1)

    place_t = lax.broadcasted_iota(jnp.int32, (d, d), 0)
    place_s = lax.broadcasted_iota(jnp.int32, (d, d), 1)
    causal = place_t >= place_s

    def columns(h):
        return pl.ds(pl.multiple_of(h * d, d), d)

    def heads_of(g, stage):
        def outer(rel):
            part = rel * core + (1 - rel) * (1 - core)

            def inner(j):
                todo = []
                for e in range(PAIR):
                    i = j * PAIR + e
                    slot = g * hc + i
                    todo.append(stage(rel, i, slot, rel * half + slot, part * half + slot))
                while todo:
                    todo = [t for t in todo if next(t, None) is not None]

            loop(0, hc // PAIR, inner)

        loop(0, 2, outer)

    def send_term(phase, rel, slot, u):
        @pl.when(rel == 0)
        def _():
            remote(r["own"].at[phase, u], r["xr"].at[phase, slot], r["xs_sem"].at[phase, slot],
                   r["xr_sem"].at[phase, slot], sibling).start()

    def features(g):
        def stage(rel, i, slot, u, h):
            w = r["wv"][h]
            val = r["vv"][:, columns(h)]
            k_pre = nn(r["kv"][:, columns(h)], w)
            yield 1
            k_feat = jnp.where(k_pre > 0, k_pre + 1.0, jnp.exp(jnp.minimum(k_pre, 0.0)))
            kf = k_feat.astype(BF16)
            r["kf"][u] = kf
            r["dk"][u] = jnp.minimum(k_feat, 1.0)
            yield 1
            r["own"][0, u] = tn(kf, val)
            r["ksown"][0, rel, g, pl.ds(i, 1), :] = jnp.sum(kf.astype(F32), axis=0, keepdims=True)
            yield 1
            send_term(0, rel, slot, u)
            yield 1
            q_pre = nn(r["qv"][:, columns(h)], w)
            yield 1
            q_feat = jnp.where(q_pre > 0, q_pre + 1.0, jnp.exp(jnp.minimum(q_pre, 0.0)))
            r["qf"][u] = q_feat.astype(BF16)
            r["dq"][u] = jnp.minimum(q_feat, 1.0)

        heads_of(g, stage)
        send_keysum(0, g)

    def send_keysum(phase, g):
        remote(r["ksown"].at[phase, 0, g], r["xk"].at[phase, g], r["xks_sem"].at[phase, g],
               r["xkr_sem"].at[phase, g], sibling).start()

    def combine(phase, g):
        tiles = hc + 1 if phase < 2 else hc

        def one(i):
            wait_for(r["xr"].at[phase, g * hc + i], r["xr_sem"].at[phase, g * hc + i])
            r["comb"][phase, g, i] = r["own"][phase, half + g * hc + i] + r["xr"][phase, g * hc + i]

        loop(0, hc, one)
        if phase < 2:
            wait_for(r["xk"].at[phase, g], r["xkr_sem"].at[phase, g])
            total = r["ksown"][phase, 1, g] + r["xk"][phase, g]
            r["comb"][phase, g, hc] = jnp.concatenate([total] * (d // 8), axis=0)

        def send(step):
            to = peer(step)
            remote(r["comb"].at[phase, g, pl.ds(0, tiles), rows_of(to), :],
                   r["recv"].at[phase, g, chip, pl.ds(0, tiles)],
                   r["as_sem"].at[phase, g], r["ar_sem"].at[phase, g], (z, to * 2 + core)).start()

        loop(1, n, send)
        r["recv"][phase, g, chip, 0:tiles] = r["comb"][phase, g, 0:tiles, rows_of(chip), :]

    def wait_rows(phase, g, sem):
        tiles = hc + 1 if phase < 2 else hc
        wait_for(r["recv"].at[phase, g, pl.ds(0, n - 1), pl.ds(0, tiles)], sem)

    def scan(phase, g):
        wait_rows(phase, g, r["ar_sem"].at[phase, g])
        recv = r["recv"]
        acc = jnp.zeros((hc, rows, d), F32)
        ks = jnp.zeros((8, d), F32)
        for i in range(n) if phase == 0 else reversed(range(n)):
            now = recv[phase, g, i, 0:hc]
            recv[phase, g, i, 0:hc] = acc
            acc = acc + now
            before = (chip > i) if phase == 0 else (chip < i)
            ks = ks + jnp.where(before, recv[phase, g, i, hc, 0:8, :], 0.0)

        def send(step):
            to = peer(step)
            remote(recv.at[phase, g, to, pl.ds(0, hc)],
                   r["back"].at[phase, g, :, rows_of(chip), :],
                   r["bs_sem"].at[phase, g], r["br_sem"].at[phase, g, chip], (z, to * 2 + core)).start()

        loop(1, n, send)
        r["back"][phase, g, :, rows_of(chip), :] = recv[phase, g, chip, 0:hc]
        mine = coref if phase == 0 else 1.0 - coref
        r["kstate"][phase, 1, g] = ks + mine * r["xk"][phase, g]
        r["ksib"][phase, g] = ks + (1.0 - mine) * r["ksown"][phase, 1, g]
        remote(r["ksib"].at[phase, g], r["kstate"].at[phase, 0, g], r["yks_sem"].at[phase, g],
               r["ykr_sem"].at[phase, g], sibling).start()

    def share(phase, g):
        mine = coref if phase == 0 else 1.0 - coref

        def one(step):
            owner = source(step)

            @pl.when(step > 0)
            def _():
                wait_for(r["back"].at[phase, g, :, rows_of(owner), :], r["br_sem"].at[phase, g, owner])

            at = rows_of(owner)
            part = r["back"][phase, g, :, at, :]
            own = r["own"][phase, pl.ds(half + g * hc, hc), at, :]
            other = r["xr"][phase, pl.ds(g * hc, hc), at, :]
            r["state"][phase, pl.ds(half + g * hc, hc), at, :] = part + mine * other
            r["sib"][phase, g, :, at, :] = part + (1.0 - mine) * own
            remote(r["sib"].at[phase, g, :, at, :], r["state"].at[phase, pl.ds(g * hc, hc), at, :],
                   r["ys_sem"].at[phase, g], r["yr_sem"].at[phase, g], sibling).start()

        loop(0, n, one)

    def shared(phase, g):
        wait_for(r["state"].at[phase, pl.ds(g * hc, hc)], r["yr_sem"].at[phase, g])
        wait_for(r["kstate"].at[phase, 0, g], r["ykr_sem"].at[phase, g])

    def local_scores(g):
        def stage(rel, i, slot, u, h):
            scores = nt(r["qf"][u], r["kf"][u])
            yield 1
            scores = jnp.where(causal, scores, 0.0)
            r["denom"][u] = jnp.sum(scores, axis=1, keepdims=True)
            low = scores.astype(BF16)
            r["sc"][u] = low
            yield 1
            r["numer"][u] = nn(low, r["vv"][:, columns(h)])

        heads_of(g, stage)

    def attend(g):
        shared(0, g)

        def stage(rel, i, slot, u, h):
            qf = r["qf"][u]
            grad = r["gv"][:, columns(h)].astype(F32)
            keysum = r["kstate"][0, rel, g, pl.ds(i, 1), :]
            numer = r["numer"][u] + nn(qf, r["state"][0, u].astype(BF16))
            qff = qf.astype(F32)
            denom = r["denom"][u] + jnp.sum(qff * keysum, axis=1, keepdims=True)
            yield 1
            inv = 1.0 / denom
            scaled = (grad * inv).astype(BF16)
            r["scaled"][u] = scaled
            wden = -jnp.sum(grad * (numer * inv), axis=1, keepdims=True) * inv
            r["wden"][u] = wden
            yield 1
            r["own"][1, u] = tn(qf, scaled)
            r["ksown"][1, rel, g, pl.ds(i, 1), :] = jnp.sum(wden * qff, axis=0, keepdims=True)
            yield 1
            send_term(1, rel, slot, u)

        heads_of(g, stage)
        send_keysum(1, g)

    def query_side(g):
        def stage(rel, i, slot, u, h):
            wden = r["wden"][u]
            scaled = r["scaled"][u]
            kf = r["kf"][u]
            keysum = r["kstate"][0, rel, g, pl.ds(i, 1), :]
            mixed = nt(scaled, r["vv"][:, columns(h)])
            yield 1
            mixed = jnp.where(causal, mixed + wden, 0.0).astype(BF16)
            yield 1
            grad = nn(mixed, kf) + nt(scaled, r["state"][0, u].astype(BF16)) + wden * keysum
            yield 1
            pre = (grad * r["dq"][u]).astype(BF16)
            yield 1
            r["qo"][:, columns(h)] = nt(pre, r["wv"][h]).astype(BF16)
            r["own"][2, u] = tn(r["qv"][:, columns(h)], pre)
            yield 1
            r["kpart"][u] = tn(mixed, r["qf"][u])
            r["vpart"][u] = tn(r["sc"][u], scaled)

        heads_of(g, stage)

    def key_side(g):
        shared(1, g)

        def stage(rel, i, slot, u, h):
            later = r["state"][1, u].astype(BF16)
            latersum = r["kstate"][1, rel, g, pl.ds(i, 1), :]
            grad = r["kpart"][u] + nt(r["vv"][:, columns(h)], later) + latersum
            yield 1
            pre = (grad * r["dk"][u]).astype(BF16)
            yield 1
            r["own"][2, u] = r["own"][2, u] + tn(r["kv"][:, columns(h)], pre)
            yield 1
            send_term(2, rel, slot, u)
            yield 1
            r["ko"][:, columns(h)] = nt(pre, r["wv"][h]).astype(BF16)
            r["vo"][:, columns(h)] = (r["vpart"][u] + nn(r["kf"][u], later)).astype(BF16)

        heads_of(g, stage)

    def sum_chips(g):
        wait_rows(2, g, r["ar_sem"].at[2, g])
        acc = r["recv"][2, g, 0, 0:hc]
        for i in range(1, n):
            acc = acc + r["recv"][2, g, i, 0:hc]
        r["tsum"][g] = acc

        def send(step):
            to = lax.rem(z + step, s.nz)
            remote(r["tsum"].at[g, lax.rem(to, hc)], r["zr"].at[g, z], r["z1s_sem"].at[g],
                   r["z1r_sem"].at[g], (to, ctx)).start()

        loop(1, s.nz, send)
        r["zr"][g, z] = r["tsum"][g, lax.rem(z, hc)]

    def sum_docs(g):
        wait_for(r["zr"].at[g, pl.ds(0, s.nz - 1)], r["z1r_sem"].at[g])
        acc = r["zr"][g, 0]
        for i in range(1, s.nz):
            acc = acc + r["zr"][g, i]
        tile = lax.rem(z, hc)
        r["fin"][g, tile] = acc
        for off in range(-(hc // 2), hc - hc // 2):
            if off != 0:
                to = lax.rem(z + s.nz + off, s.nz)
                remote(r["fin"].at[g, tile], r["fin"].at[g, tile], r["z2s_sem"].at[g],
                       r["z2r_sem"].at[g], (to, ctx)).start()

    def to_sibling(g, owner):
        heads = pl.ds(core * half + g * hc, hc)
        block = r["mo"].at[heads, rows_of(owner), :]
        remote(block, block, r["ys_sem"].at[2, g], r["yr_sem"].at[2, g], sibling).start()

    def spread(g):
        heads = pl.ds(core * half + g * hc, hc)
        wait_for(r["fin"].at[g, pl.ds(0, hc - 1)], r["z2r_sem"].at[g])

        def send(step):
            to = peer(step)
            remote(r["fin"].at[g], r["mo"].at[heads, rows_of(chip), :], r["bs_sem"].at[2, g],
                   r["br_sem"].at[2, g, chip], (z, to * 2 + core)).start()

        loop(1, n, send)
        r["mo"][heads, rows_of(chip), :] = r["fin"][g]
        to_sibling(g, chip)

    def collect(g):
        heads = pl.ds(core * half + g * hc, hc)

        def one(step):
            owner = source(step)
            wait_for(r["mo"].at[heads, rows_of(owner), :], r["br_sem"].at[2, g, owner])
            to_sibling(g, owner)

        loop(1, n, one)

    groups = range(s.groups)
    for g in groups:
        features(g)
        if g > 0:
            combine(0, g - 1)
    combine(0, s.groups - 1)
    for g in groups:
        local_scores(g)
        scan(0, g)
    loads[4].wait()
    for g in groups:
        share(0, g)
        attend(g)
        if g > 0:
            combine(1, g - 1)
    combine(1, s.groups - 1)
    for g in groups:
        query_side(g)
        scan(1, g)
    stores = [pltpu.make_async_copy(r["qo"], qg_hbm.at[0], r["out_sem"].at[0])]
    stores[0].start()
    for g in groups:
        share(1, g)
        key_side(g)
        if g > 0:
            combine(2, g - 1)
    combine(2, s.groups - 1)
    stores.append(pltpu.make_async_copy(r["ko"], kg_hbm.at[0], r["out_sem"].at[1]))
    stores.append(pltpu.make_async_copy(r["vo"], vg_hbm.at[0], r["out_sem"].at[2]))
    stores[1].start()
    stores[2].start()
    for g in groups:
        sum_chips(g)
    for g in groups:
        sum_docs(g)
    for g in groups:
        spread(g)
    for g in groups:
        collect(g)
    other = (1 - core) * half
    for g in groups:
        wait_for(r["mo"].at[pl.ds(other + g * hc, hc)], r["yr_sem"].at[2, g])
    stores.append(pltpu.make_async_copy(r["mo"], mg_hbm, r["out_sem"].at[3]))
    stores[3].start()

    for phase in range(3):
        tiles = hc + 1 if phase < 2 else hc
        for slot in range(half):
            wait_for(r["own"].at[phase, slot], r["xs_sem"].at[phase, slot])
        for g in groups:
            wait_for(r["recv"].at[phase, g, pl.ds(0, n - 1), pl.ds(0, tiles)], r["as_sem"].at[phase, g])
            wait_for(r["recv"].at[phase, g, pl.ds(0, n - 1), pl.ds(0, hc)], r["bs_sem"].at[phase, g])
            wait_for(r["mo"].at[pl.ds(0, hc)], r["ys_sem"].at[phase, g])
            if phase < 2:
                wait_for(r["xk"].at[phase, g], r["xks_sem"].at[phase, g])
                wait_for(r["ksib"].at[phase, g], r["yks_sem"].at[phase, g])
    for g in groups:
        wait_for(r["zr"].at[g, pl.ds(0, s.nz - 1)], r["z1s_sem"].at[g])
        wait_for(r["fin"].at[g, pl.ds(0, hc - 1)], r["z2s_sem"].at[g])
    for store in stores:
        store.wait()


def solution(mesh):
    nz, nctx = mesh.shape["dp"], mesh.shape["ctx"]

    def per_device(queries, keys, values, out_grad, map_weight):
        heads, dim = map_weight.shape[0], map_weight.shape[1]
        s = Sizes(nz, nctx, heads, dim)
        spaces = scratch(s)
        act = jax.ShapeDtypeStruct(queries.shape, BF16)
        return pl.pallas_call(
            functools.partial(kernel, s, tuple(spaces)),
            out_shape=(act, act, act, jax.ShapeDtypeStruct(map_weight.shape, F32)),
            in_specs=[pl.BlockSpec(memory_space=pl.ANY)] * 5,
            out_specs=(pl.BlockSpec(memory_space=pl.ANY),) * 4,
            scratch_shapes=list(spaces.values()),
            compiler_params=pltpu.CompilerParams(
                collective_id=0, has_side_effects=True, vmem_limit_bytes=48 * 1024 * 1024),
            cost_estimate=pl.CostEstimate(
                flops=36 * heads * dim**3, bytes_accessed=5 * 1024 * 1024, transcendentals=2 * heads * dim**2),
        )(queries, keys, values, out_grad, map_weight)

    split = P("dp", "ctx", None)
    return jax.shard_map(
        per_device, mesh=mesh, in_specs=(split, split, split, split, P()),
        out_specs=(split, split, split, P()), check_vma=False)
```

time: 856 us -> 103 us (0.12)
  waiting for transfers between devices: 652 us -> 0 us
  blocking collectives: 96.8 us -> 0 us
  Pallas kernels: 0 us -> 93.2 us
  other arithmetic: 47.9 us -> 0 us
  matrix products: 29 us -> 0 us
  between operations: 14 us -> 0.65 us
    psum x1 -> x0, waiting for transfers between devices: 461 us -> none  [per_device(): map_total = lax.psum(map_local, ('dp', 'ctx'))]
    all_gather x2 -> x0, waiting for transfers between devices: 192 us -> none  [prefix(): gathered = jax.tree.map(lambda a: lax.all_gather(a, axis), part)]
    all_gather x2 -> x0, blocking collectives: 96.8 us -> none  [prefix(): gathered = jax.tree.map(lambda a: lax.all_gather(a, axis), part)]
    pallas_call x0 -> x1, Pallas kernels: none -> 93.2 us  [per_device(): pl.pallas_call(functools.partial(kernel, s, tuple(spaces)), out_shape=(ac...]
    add x63 -> x0, other arithmetic: 46.5 us -> none  [the longest x62 46.5 us: add_pair(): return (earlier[0] + later[0], earlier[1] + later[1])]
    dot_general x20 -> x0, matrix products: 29 us -> none  [the longest x18 27.6 us: lowmult(): return jnp.einsum(form, left, right, preferred_element_type=jnp.float32)]
  transfers between devices with their start and end apart: 3 -> 0, of which waited for: 3 -> 0; matrix products, arithmetic and copies ran while one was open for 3% -> 0% of each run, Pallas kernels for 0% -> 0%
where the time goes in v1:
time: 103 us; the launch traced here: 102 us
  Pallas kernels  93.2 us (90%)
  local copies, waits for them, and re-layouts  8.55 us (8%)
    pallas_call x1, Pallas kernels, per_device(): pl.pallas_call(functools.partial(kernel, s, tuple(spaces)), out_shape=(ac...  93.2 us
    unnamed x14, local copies, waits for them, and re-layouts  8.55 us

profile of v1, /device:TPU:1, one launch (start us, length us, event | category | flops | bytes accessed | tf_op | source)
XLA Modules:
  0.0 102.4 jit_solution(9701003693103022338)
XLA Ops:
  0.6 0.0 copy-start
  0.6 1.0 %copy-done = bf16[1,128,2048]{2,1,0:T(8,128)(2,1)S(1)} copy-done((bf16[1,128,2048]{2,1,0:T(8,128)(2,1)S(1)}, bf16[1,128,2048]{2,1,0:T(8,128)(2,1)}, u32[]{:S(2)}) %copy-start) | copy-done | bytes 524312
  1.7 0.0 copy-start.1
  1.7 1.0 %copy-done.1 = bf16[1,128,2048]{2,1,0:T(8,128)(2,1)S(1)} copy-done((bf16[1,128,2048]{2,1,0:T(8,128)(2,1)S(1)}, bf16[1,128,2048]{2,1,0:T(8,128)(2,1)}, u32[]{:S(2)}) %copy-start.1) | copy-done | bytes 524312
  2.7 0.0 copy-start.2
  2.7 1.0 %copy-done.2 = bf16[1,128,2048]{2,1,0:T(8,128)(2,1)S(1)} copy-done((bf16[1,128,2048]{2,1,0:T(8,128)(2,1)S(1)}, bf16[1,128,2048]{2,1,0:T(8,128)(2,1)}, u32[]{:S(2)}) %copy-start.2) | copy-done | bytes 524312
  3.8 0.0 copy-start.3
  3.8 1.0 %copy-done.3 = bf16[1,128,2048]{2,1,0:T(8,128)(2,1)S(1)} copy-done((bf16[1,128,2048]{2,1,0:T(8,128)(2,1)S(1)}, bf16[1,128,2048]{2,1,0:T(8,128)(2,1)}, u32[]{:S(2)}) %copy-start.3) | copy-done | bytes 524312
  4.8 0.0 copy-start.4
  4.8 1.0 %copy-done.4 = bf16[16,128,128]{2,1,0:T(8,128)(2,1)S(1)} copy-done((bf16[16,128,128]{2,1,0:T(8,128)(2,1)S(1)}, bf16[16,128,128]{2,1,0:T(8,128)(2,1)}, u32[]{:S(2)}) %copy-start.4) | copy-done | bytes 524312
  5.8 93.2 %shard_map.84 = (bf16[1,128,2048]{2,1,0:T(8,128)(2,1)S(1)}, bf16[1,128,2048]{2,1,0:T(8,128)(2,1)S(1)}, bf16[1,128,2048]{2,1,0:T(8,128)(2,1)S(1)}, f32[16,128,128]{2,1,0:T(8,128)S(1)}) custom-call(bf16[1,128,2048]{2,1,0:T(8,128)(2,1)S(1)} %copy-done, bf16[1,128,2048]{2,1,0:T(8,128)(2,1)S(1)} %copy-done.1, bf16[1,128,2048]{2,1,0:T(8,128)(2,1)S(1)} %copy-done.2, ...), custom_call_target="tpu_custom_call" | custom-call | flops 1207959552 | bytes 5242880 | tf_op jit(solution)/shard_map/pallas_call | solution.py:474
  99.1 0.8 copy.13
  99.9 0.8 copy.14
  100.7 0.8 copy.15
  101.5 1.0 copy.16
Async XLA Ops:
  0.6 1.0 %copy-start = (bf16[1,128,2048]{2,1,0:T(8,128)(2,1)S(1)}, bf16[1,128,2048]{2,1,0:T(8,128)(2,1)}, u32[]{:S(2)}) copy-start(bf16[1,128,2048]{2,1,0:T(8,128)(2,1)} %q_hbm.1) | copy-start | bytes 1572868
  1.7 1.0 %copy-start.1 = (bf16[1,128,2048]{2,1,0:T(8,128)(2,1)S(1)}, bf16[1,128,2048]{2,1,0:T(8,128)(2,1)}, u32[]{:S(2)}) copy-start(bf16[1,128,2048]{2,1,0:T(8,128)(2,1)} %k_hbm.1) | copy-start | bytes 1572868
  2.7 1.0 %copy-start.2 = (bf16[1,128,2048]{2,1,0:T(8,128)(2,1)S(1)}, bf16[1,128,2048]{2,1,0:T(8,128)(2,1)}, u32[]{:S(2)}) copy-start(bf16[1,128,2048]{2,1,0:T(8,128)(2,1)} %v_hbm.1) | copy-start | bytes 1572868
  3.8 1.0 %copy-start.3 = (bf16[1,128,2048]{2,1,0:T(8,128)(2,1)S(1)}, bf16[1,128,2048]{2,1,0:T(8,128)(2,1)}, u32[]{:S(2)}) copy-start(bf16[1,128,2048]{2,1,0:T(8,128)(2,1)} %g_hbm.1) | copy-start | bytes 1572868
  4.8 1.0 %copy-start.4 = (bf16[16,128,128]{2,1,0:T(8,128)(2,1)S(1)}, bf16[16,128,128]{2,1,0:T(8,128)(2,1)}, u32[]{:S(2)}) copy-start(bf16[16,128,128]{2,1,0:T(8,128)(2,1)} %w_hbm.1) | copy-start | bytes 1572868

commit v2 on v0

v2 whole, which is shorter than its diff:
```python
import functools
import math

import jax
import jax.numpy as jnp
from jax import lax
from jax.experimental import pallas as pl
from jax.experimental.pallas import tpu as pltpu
from jax.sharding import PartitionSpec as P

GROUPS = 2
F32 = jnp.float32
BF16 = jnp.bfloat16


def nn(a, b):
    return lax.dot_general(a, b, (((1,), (0,)), ((), ())), preferred_element_type=F32)


def nt(a, b):
    return lax.dot_general(a, b, (((1,), (1,)), ((), ())), preferred_element_type=F32)


def tn(a, b):
    return lax.dot_general(a, b, (((0,), (0,)), ((), ())), preferred_element_type=F32)


class Sizes:
    def __init__(self, nz, nctx, heads, dim):
        self.nz = nz
        self.chips = nctx // 2
        self.ny = math.isqrt(self.chips)
        self.heads = heads
        self.half = heads // 2
        self.groups = GROUPS
        self.hc = self.half // GROUPS
        self.dim = dim
        self.rows = dim // self.chips
        near = lambda a, size: min(a, size - a)
        self.plane = sorted(
            ((a, b) for a in range(self.ny) for b in range(self.ny) if a or b),
            key=lambda t: -near(t[0], self.ny) - near(t[1], self.ny))
        self.along = sorted(range(1, nz), key=lambda a: -near(a, nz))


def scratch(s):
    d, hc, g, n, hf = s.dim, s.hc, s.groups, s.chips, s.half
    dma = pltpu.SemaphoreType.DMA
    v = pltpu.VMEM
    wide = hf * d
    return dict(
        xin=v((4, 2, d, wide), BF16), xout=v((4, d, wide), BF16), wv=v((hf, d, d), BF16),
        swap=v((4, d, wide), F32), got=v((4, d, wide), F32),
        qf=v((2, hf, d, d), BF16), kf=v((2, hf, d, d), BF16),
        dq=v((2, hf, d, d), F32), dk=v((2, hf, d, d), F32),
        sc=v((2, hf, d, d), BF16), scaled=v((2, hf, d, d), BF16), kpre=v((2, hf, d, d), BF16),
        numer=v((2, hf, d, d), F32), denom=v((2, hf, d, 1), F32), wden=v((2, hf, d, 1), F32),
        kpart=v((2, hf, d, d), F32), vpart=v((2, hf, d, d), F32),
        own=v((3, 2, hf, d, d), F32), ksown=v((2, 2, g, 8, d), F32),
        comb=v((3, g, hc + 1, d, d), F32), recv=v((3, g, n, hc + 1, s.rows, d), F32),
        back=v((2, g, hc, d, d), F32), kback=v((2, g, 8, d), F32),
        tsum=v((g, hc, s.rows, d), F32), zr=v((g, s.nz, s.rows, d), F32), fin=v((g, hc, s.rows, d), F32),
        outs=v((3, 2, d, wide), F32), outr=v((3, d, wide), F32),
        in_sem=dma((9,)), sws_sem=dma((4,)), swr_sem=dma((4,)), os_sem=dma((3,)), or_sem=dma((3,)),
        as_sem=dma((3, g)), ar_sem=dma((3, g)),
        bs_sem=dma((3, g)), br_sem=dma((2, g)), mr_sem=dma((g, s.ny)),
        ys_sem=dma((g,)), yr_sem=dma((g,)),
        z1s_sem=dma((g,)), z1r_sem=dma((g,)), z2s_sem=dma((g,)), z2r_sem=dma((g,)),
    )


KEY, VALUE, QUERY, GRAD = range(4)


def kernel(s, names, q_hbm, k_hbm, v_hbm, g_hbm, w_hbm, qo, ko, vo, mo, *refs):
    r = dict(zip(names, refs))
    n, hc, d, half, rows, ny = s.chips, s.hc, s.dim, s.half, s.rows, s.ny
    wide = half * d
    z = lax.axis_index("dp")
    ctx = lax.axis_index("ctx")
    core = lax.rem(ctx, 2)
    chip = lax.div(ctx, 2)
    cx, cy = lax.div(chip, ny), lax.rem(chip, ny)
    sibling = (z, chip * 2 + 1 - core)
    groups = range(s.groups)

    def wrap(a, size):
        return jnp.where(a >= size, a - size, a)

    peers = [wrap(cx + a, ny) * ny + wrap(cy + b, ny) for a, b in s.plane]
    depths = [wrap(z + a, s.nz) for a in s.along]

    def remote(src, dst, send, recv, device):
        return pltpu.make_async_remote_copy(
            src_ref=src, dst_ref=dst, send_sem=send, recv_sem=recv, device_id=device,
            device_id_type=pl.DeviceIdType.MESH)

    def wait_for(ref, sem):
        pltpu.make_async_copy(ref, ref, sem).wait()

    def rows_of(owner):
        return pl.ds(pl.multiple_of(owner * rows, rows), rows)

    def half_of(which):
        return pl.ds(pl.multiple_of(which * wide, wide), wide)

    barrier = pltpu.get_barrier_semaphore()

    def greet(device):
        pl.semaphore_signal(barrier, inc=1, device_id=device, device_id_type=pl.DeviceIdType.MESH)

    for to in depths:
        greet((to, ctx))
    for to in peers:
        greet((z, to * 2 + core))
    greet(sibling)

    inputs = (k_hbm, v_hbm, q_hbm, g_hbm)
    away = [pltpu.make_async_copy(x.at[0, :, half_of(1 - core)], r["xout"].at[a], r["in_sem"].at[a])
            for a, x in enumerate(inputs)]
    home = [pltpu.make_async_copy(x.at[0, :, half_of(core)], r["xin"].at[a, core], r["in_sem"].at[4 + a])
            for a, x in enumerate(inputs)]
    load_w = pltpu.make_async_copy(
        w_hbm.at[pl.ds(core * half, half)], r["wv"], r["in_sem"].at[8])
    for load in (away[KEY], away[VALUE], load_w, home[KEY], home[VALUE], away[QUERY], away[GRAD], home[QUERY],
                 home[GRAD]):
        load.start()
    r["ksown"][...] = jnp.zeros_like(r["ksown"])

    def swap_out(a):
        away[a].wait()
        r["swap"][a] = r["xout"][a].astype(F32)

    def swap_send(a):
        for part in range(2):
            at = pl.ds(part * (d // 2), d // 2)
            remote(r["swap"].at[a, at], r["got"].at[a, at], r["sws_sem"].at[a], r["swr_sem"].at[a], sibling).start()

    def swap_in(a):
        wait_for(r["got"].at[a], r["swr_sem"].at[a])
        r["xin"][a, 1 - core] = r["got"][a].astype(BF16)

    place_t = lax.broadcasted_iota(jnp.int32, (d, d), 0)
    place_s = lax.broadcasted_iota(jnp.int32, (d, d), 1)
    causal = place_t >= place_s

    def block(a, b, u):
        return r["xin"][a, b, :, u * d:(u + 1) * d]

    def heads_of(g, stage, blocks=(0, 1)):
        todo = [stage(b, i, g * hc + i) for b in blocks for i in range(hc)]
        while todo:
            todo = [t for t in todo if next(t, None) is not None]

    def key_features(g, b):
        def stage(b, i, u):
            k_pre = nn(block(KEY, b, u), r["wv"][u])
            yield 1
            k_feat = jnp.where(k_pre > 0, k_pre + 1.0, jnp.exp(jnp.minimum(k_pre, 0.0)))
            kf = k_feat.astype(BF16)
            r["kf"][b, u] = kf
            r["dk"][b, u] = jnp.minimum(k_feat, 1.0)
            yield 1
            r["own"][0, b, u] = tn(kf, block(VALUE, b, u))
            r["ksown"][0, b, g, i:i + 1, :] = jnp.sum(kf.astype(F32), axis=0, keepdims=True)

        heads_of(g, stage, (b,))

    def send_rows(phase, g):
        tiles = hc + 1 if phase < 2 else hc
        for i in range(hc):
            u = g * hc + i
            r["comb"][phase, g, i] = r["own"][phase, 0, u] + r["own"][phase, 1, u]
        if phase < 2:
            total = r["ksown"][phase, 0, g] + r["ksown"][phase, 1, g]
            r["comb"][phase, g, hc] = jnp.concatenate([total] * (d // 8), axis=0)
        for to in peers:
            remote(r["comb"].at[phase, g, pl.ds(0, tiles), rows_of(to), :],
                   r["recv"].at[phase, g, chip, pl.ds(0, tiles)],
                   r["as_sem"].at[phase, g], r["ar_sem"].at[phase, g], (z, to * 2 + core)).start()
        r["recv"][phase, g, chip, 0:tiles] = r["comb"][phase, g, 0:tiles, rows_of(chip), :]

    def wait_rows(phase, g, sem):
        tiles = hc + 1 if phase < 2 else hc
        wait_for(r["recv"].at[phase, g, pl.ds(0, n - 1), pl.ds(0, tiles)], sem)

    def scan(phase, g):
        wait_rows(phase, g, r["ar_sem"].at[phase, g])
        recv = r["recv"]
        acc = jnp.zeros((hc, rows, d), F32)
        for i in range(n) if phase == 0 else reversed(range(n)):
            now = recv[phase, g, i, 0:hc]
            recv[phase, g, i, 0:hc] = acc
            acc = acc + now
        for to in peers:
            remote(recv.at[phase, g, to, pl.ds(0, hc)],
                   r["back"].at[phase, g, :, rows_of(chip), :],
                   r["bs_sem"].at[phase, g], r["br_sem"].at[phase, g], (z, to * 2 + core)).start()
        r["back"][phase, g, :, rows_of(chip), :] = recv[phase, g, chip, 0:hc]
        ks = jnp.zeros((8, d), F32)
        for i in range(n):
            before = (chip > i) if phase == 0 else (chip < i)
            ks = ks + jnp.where(before, recv[phase, g, i, hc, 0:8, :], 0.0)
        r["kback"][phase, g] = ks

    def returned(phase, g):
        wait_for(r["back"].at[phase, g, :, pl.ds(0, (n - 1) * rows), :], r["br_sem"].at[phase, g])

    def state_of(phase, b, g, i):
        state = r["back"][phase, g, i]
        if b != phase:
            state = state + r["own"][phase, phase, g * hc + i]
        return state.astype(BF16)

    def sum_of(phase, b, g, i):
        total = r["kback"][phase, g, i:i + 1, :]
        if b != phase:
            total = total + r["ksown"][phase, phase, g, i:i + 1, :]
        return total

    def local_scores(g, blocks=(0, 1)):
        def stage(b, i, u):
            q_pre = nn(block(QUERY, b, u), r["wv"][u])
            yield 1
            q_feat = jnp.where(q_pre > 0, q_pre + 1.0, jnp.exp(jnp.minimum(q_pre, 0.0)))
            qf = q_feat.astype(BF16)
            r["qf"][b, u] = qf
            r["dq"][b, u] = jnp.minimum(q_feat, 1.0)
            yield 1
            scores = nt(qf, r["kf"][b, u])
            yield 1
            scores = jnp.where(causal, scores, 0.0)
            r["denom"][b, u] = jnp.sum(scores, axis=1, keepdims=True)
            low = scores.astype(BF16)
            r["sc"][b, u] = low
            yield 1
            r["numer"][b, u] = nn(low, block(VALUE, b, u))

        heads_of(g, stage, blocks)

    def attend(g):
        def stage(b, i, u):
            qf = r["qf"][b, u]
            grad = block(GRAD, b, u).astype(F32)
            numer = r["numer"][b, u] + nn(qf, state_of(0, b, g, i))
            qff = qf.astype(F32)
            denom = r["denom"][b, u] + jnp.sum(qff * sum_of(0, b, g, i), axis=1, keepdims=True)
            yield 1
            inv = 1.0 / denom
            scaled = (grad * inv).astype(BF16)
            r["scaled"][b, u] = scaled
            wden = -jnp.sum(grad * (numer * inv), axis=1, keepdims=True) * inv
            r["wden"][b, u] = wden
            yield 1
            r["own"][1, b, u] = tn(qf, scaled)
            r["ksown"][1, b, g, i:i + 1, :] = jnp.sum(wden * qff, axis=0, keepdims=True)

        heads_of(g, stage)

    def query_side(g, blocks=(0, 1)):
        def stage(b, i, u):
            wden = r["wden"][b, u]
            scaled = r["scaled"][b, u]
            mixed = nt(scaled, block(VALUE, b, u))
            yield 1
            mixed = jnp.where(causal, mixed + wden, 0.0).astype(BF16)
            yield 1
            grad = nn(mixed, r["kf"][b, u]) + nt(scaled, state_of(0, b, g, i)) + wden * sum_of(0, b, g, i)
            yield 1
            pre = (grad * r["dq"][b, u]).astype(BF16)
            yield 1
            r["outs"][0, b, :, u * d:(u + 1) * d] = nt(pre, r["wv"][u])
            r["own"][2, b, u] = tn(block(QUERY, b, u), pre)
            yield 1
            r["kpart"][b, u] = tn(mixed, r["qf"][b, u])
            r["vpart"][b, u] = tn(r["sc"][b, u], scaled)

        heads_of(g, stage, blocks)

    def key_side(g):
        def stage(b, i, u):
            grad = r["kpart"][b, u] + nt(block(VALUE, b, u), state_of(1, b, g, i)) + sum_of(1, b, g, i)
            yield 1
            pre = (grad * r["dk"][b, u]).astype(BF16)
            r["kpre"][b, u] = pre
            yield 1
            r["own"][2, b, u] = r["own"][2, b, u] + tn(block(KEY, b, u), pre)

        heads_of(g, stage)

    def key_outputs(g):
        def stage(b, i, u):
            r["outs"][1, b, :, u * d:(u + 1) * d] = nt(r["kpre"][b, u], r["wv"][u])
            r["outs"][2, b, :, u * d:(u + 1) * d] = r["vpart"][b, u] + nn(r["kf"][b, u], state_of(1, b, g, i))
            yield 1

        heads_of(g, stage)

    def give_out(a):
        remote(r["outs"].at[a, 1 - core], r["outr"].at[a], r["os_sem"].at[a], r["or_sem"].at[a], sibling).start()
        (qo, ko, vo)[a][0, :, half_of(core)] = r["outs"][a, core].astype(BF16)

    def take_out(a):
        wait_for(r["outr"].at[a], r["or_sem"].at[a])
        (qo, ko, vo)[a][0, :, half_of(1 - core)] = r["outr"][a].astype(BF16)

    def sum_chips(g):
        wait_rows(2, g, r["ar_sem"].at[2, g])
        acc = r["recv"][2, g, 0, 0:hc]
        for i in range(1, n):
            acc = acc + r["recv"][2, g, i, 0:hc]
        r["tsum"][g] = acc
        for to in depths:
            remote(r["tsum"].at[g, lax.rem(to, hc)], r["zr"].at[g, z], r["z1s_sem"].at[g],
                   r["z1r_sem"].at[g], (to, ctx)).start()
        r["zr"][g, z] = r["tsum"][g, lax.rem(z, hc)]

    def sum_docs(g):
        wait_for(r["zr"].at[g, pl.ds(0, s.nz - 1)], r["z1r_sem"].at[g])
        acc = r["zr"][g, 0]
        for i in range(1, s.nz):
            acc = acc + r["zr"][g, i]
        tile = lax.rem(z, hc)
        r["fin"][g, tile] = acc
        for off in range(-(hc // 2), hc - hc // 2):
            if off != 0:
                to = wrap(z + off % s.nz, s.nz)
                remote(r["fin"].at[g, tile], r["fin"].at[g, tile], r["z2s_sem"].at[g],
                       r["z2r_sem"].at[g], (to, ctx)).start()

    def spread(g):
        heads = pl.ds(core * half + g * hc, hc)
        if hc > 1:
            wait_for(r["fin"].at[g, pl.ds(0, hc - 1)], r["z2r_sem"].at[g])
        for to in peers:
            remote(r["fin"].at[g], mo.at[heads, rows_of(chip), :], r["bs_sem"].at[2, g],
                   r["mr_sem"].at[g, cx], (z, to * 2 + core)).start()
        mo[heads, rows_of(chip), :] = r["fin"][g]

    def strips():
        order = [0] + sorted(range(1, ny), key=lambda a: min(a, ny - a))
        for a in order:
            px = wrap(cx + a, ny)
            start = pl.multiple_of(px * (ny * rows), ny * rows)
            yield px, start, (ny if a else ny - 1)

    def collect(g):
        heads = pl.ds(core * half + g * hc, hc)
        for px, start, count in strips():
            wait_for(mo.at[heads, pl.ds(start, count * rows), :], r["mr_sem"].at[g, px])
            part = mo.at[heads, pl.ds(start, ny * rows), :]
            remote(part, part, r["ys_sem"].at[g], r["yr_sem"].at[g], sibling).start()

    first, last = groups[:-1], s.groups - 1
    swap_out(KEY)
    pl.semaphore_wait(barrier, n + s.nz - 1)
    swap_send(KEY)
    swap_out(VALUE)
    swap_send(VALUE)
    load_w.wait()
    home[KEY].wait()
    home[VALUE].wait()
    swap_in(KEY)
    swap_in(VALUE)
    for g in groups:
        key_features(g, 0)
        key_features(g, 1)
        send_rows(0, g)
    for a in (QUERY, GRAD):
        swap_out(a)
        swap_send(a)
        home[a].wait()
    swap_in(QUERY)
    for g in first:
        local_scores(g)
        scan(0, g)
    local_scores(last, (0,))
    scan(0, last)
    local_scores(last, (1,))
    swap_in(GRAD)
    for g in groups:
        returned(0, g)
        attend(g)
        send_rows(1, g)
    query_side(0)
    for g in first:
        query_side(g + 1, (0,))
        scan(1, g)
        query_side(g + 1, (1,))
    scan(1, last)
    give_out(0)
    for g in groups:
        returned(1, g)
        key_side(g)
        send_rows(2, g)
    for g in groups:
        key_outputs(g)
    give_out(1)
    give_out(2)
    for g in groups:
        sum_chips(g)
    for a in range(3):
        take_out(a)
    for g in groups:
        sum_docs(g)
    for g in groups:
        spread(g)
    for g in groups:
        collect(g)
    other = (1 - core) * half
    for g in groups:
        wait_for(mo.at[pl.ds(other + g * hc, hc)], r["yr_sem"].at[g])

    for a in range(4):
        wait_for(r["got"].at[a], r["sws_sem"].at[a])
    for a in range(3):
        wait_for(r["outr"].at[a], r["os_sem"].at[a])
    for g in groups:
        for phase in range(3):
            wait_rows(phase, g, r["as_sem"].at[phase, g])
            wait_for(r["recv"].at[phase, g, pl.ds(0, n - 1), pl.ds(0, hc)], r["bs_sem"].at[phase, g])
        wait_for(mo.at[pl.ds(0, hc)], r["ys_sem"].at[g])
        wait_for(r["zr"].at[g, pl.ds(0, s.nz - 1)], r["z1s_sem"].at[g])
        if hc > 1:
            wait_for(r["fin"].at[g, pl.ds(0, hc - 1)], r["z2s_sem"].at[g])


def write_out(*refs):
    count = len(refs) // 2
    sems = refs[-1]
    copies = []
    for i, (src, dst) in enumerate(zip(refs[:count], refs[count:-1])):
        copies.append(pltpu.make_async_copy(src, dst, sems.at[i]))
    for copy in copies:
        copy.start()
    for copy in copies:
        copy.wait()


def solution(mesh):
    nz, nctx = mesh.shape["dp"], mesh.shape["ctx"]

    def per_device(queries, keys, values, out_grad, map_weight):
        heads, dim = map_weight.shape[0], map_weight.shape[1]
        s = Sizes(nz, nctx, heads, dim)
        spaces = scratch(s)
        act = jax.ShapeDtypeStruct(queries.shape, BF16)
        shapes = (act, act, act, jax.ShapeDtypeStruct(map_weight.shape, F32))
        grads = pl.pallas_call(
            functools.partial(kernel, s, tuple(spaces)),
            out_shape=shapes,
            in_specs=[pl.BlockSpec(memory_space=pltpu.HBM)] * 5,
            out_specs=(pl.BlockSpec(memory_space=pltpu.VMEM),) * 4,
            scratch_shapes=list(spaces.values()),
            compiler_params=pltpu.CompilerParams(
                collective_id=0, has_side_effects=True, vmem_limit_bytes=52 * 1024 * 1024),
            cost_estimate=pl.CostEstimate(
                flops=36 * heads * dim**3, bytes_accessed=5 * 1024 * 1024, transcendentals=2 * heads * dim**2),
        )(queries, keys, values, out_grad, map_weight)
        return pl.pallas_call(
            write_out,
            out_shape=shapes,
            in_specs=[pl.BlockSpec(memory_space=pltpu.VMEM)] * 4,
            out_specs=(pl.BlockSpec(memory_space=pltpu.HBM),) * 4,
            scratch_shapes=[pltpu.SemaphoreType.DMA((4,))],
            compiler_params=pltpu.CompilerParams(vmem_limit_bytes=4 * 1024 * 1024),
        )(*grads)

    split = P("dp", "ctx", None)
    return jax.shard_map(
        per_device, mesh=mesh, in_specs=(split, split, split, split, P()),
        out_specs=(split, split, split, P()), check_vma=False)
```

time: 856 us -> 80.1 us (0.09)
  waiting for transfers between devices: 652 us -> 0 us
  blocking collectives: 96.8 us -> 0 us
  Pallas kernels: 0 us -> 78 us
  other arithmetic: 47.9 us -> 0 us
  matrix products: 29 us -> 0 us
  between operations: 14 us -> 0.65 us
  local copies, waits for them, and re-layouts: 13 us -> 1.22 us
    psum x1 -> x0, waiting for transfers between devices: 461 us -> none  [per_device(): map_total = lax.psum(map_local, ('dp', 'ctx'))]
    all_gather x2 -> x0, waiting for transfers between devices: 192 us -> none  [prefix(): gathered = jax.tree.map(lambda a: lax.all_gather(a, axis), part)]
    all_gather x2 -> x0, blocking collectives: 96.8 us -> none  [prefix(): gathered = jax.tree.map(lambda a: lax.all_gather(a, axis), part)]
    pallas_call x0 -> x2, Pallas kernels: none -> 78 us  [the longest x1 76.5 us: per_device(): pl.pallas_call(functools.partial(kernel, s, tuple(spaces)), out_shape=sha...]
    add x63 -> x0, other arithmetic: 46.5 us -> none  [the longest x62 46.5 us: add_pair(): return (earlier[0] + later[0], earlier[1] + later[1])]
    dot_general x20 -> x0, matrix products: 29 us -> none  [the longest x18 27.6 us: lowmult(): return jnp.einsum(form, left, right, preferred_element_type=jnp.float32)]
    unnamed x19 -> x2, local copies, waits for them, and re-layouts: 10.5 us -> 1.22 us
  transfers between devices with their start and end apart: 3 -> 0, of which waited for: 3 -> 0; matrix products, arithmetic and copies ran while one was open for 3% -> 0% of each run, Pallas kernels for 0% -> 0%
where the time goes in v2:
time: 80.1 us; the launch traced here: 79.9 us
  Pallas kernels  78 us (97%)
  local copies, waits for them, and re-layouts  1.22 us (2%)
    pallas_call x1, Pallas kernels, per_device(): pl.pallas_call(functools.partial(kernel, s, tuple(spaces)), out_shape=sha...  76.5 us

profile of v2, /device:TPU:1, one launch (start us, length us, event | category | flops | bytes accessed | tf_op | source)
XLA Modules:
  0.0 79.9 jit_solution(15417383216326564593)
XLA Ops:
  0.6 76.5 %shard_map.84 = (bf16[1,128,2048]{2,1,0:T(8,128)(2,1)S(1)}, bf16[1,128,2048]{2,1,0:T(8,128)(2,1)S(1)}, bf16[1,128,2048]{2,1,0:T(8,128)(2,1)S(1)}, f32[16,128,128]{2,1,0:T(8,128)}) custom-call(bf16[1,128,2048]{2,1,0:T(8,128)(2,1)} %q_hbm.1, bf16[1,128,2048]{2,1,0:T(8,128)(2,1)} %k_hbm.1, bf16[1,128,2048]{2,1,0:T(8,128)(2,1)} %v_hbm.1, ...), custom_call_target="tpu_custom_call" | custom-call | flops 1207959552 | bytes 5242880 | tf_op jit(solution)/shard_map/pallas_call | solution.py:449
  77.2 0.0 copy-start
  77.2 1.2 %copy-done = f32[16,128,128]{2,1,0:T(8,128)S(1)} copy-done((f32[16,128,128]{2,1,0:T(8,128)S(1)}, f32[16,128,128]{2,1,0:T(8,128)}, u32[]{:S(2)}) %copy-start) | copy-done | bytes 1048600
  78.4 1.5 %shard_map.85 = (bf16[1,128,2048]{2,1,0:T(8,128)(2,1)}, bf16[1,128,2048]{2,1,0:T(8,128)(2,1)}, bf16[1,128,2048]{2,1,0:T(8,128)(2,1)}, f32[16,128,128]{2,1,0:T(8,128)}) custom-call(bf16[1,128,2048]{2,1,0:T(8,128)(2,1)S(1)} %get-tuple-element.8.refs_0_, bf16[1,128,2048]{2,1,0:T(8,128)(2,1)S(1)} %get-tuple-element.9.refs_1_, ...), custom_call_target="tpu_custom_call" | custom-call | tf_op jit(solution)/shard_map/pallas_call | solution.py:460
Async XLA Ops:
  77.2 1.2 %copy-start = (f32[16,128,128]{2,1,0:T(8,128)S(1)}, f32[16,128,128]{2,1,0:T(8,128)}, u32[]{:S(2)}) copy-start(f32[16,128,128]{2,1,0:T(8,128)} %get-tuple-element.11.refs_3_) | copy-start | bytes 3145732

commit v3 on v2

--- a/solution.py
+++ b/solution.py
@@ -56,12 +56,12 @@
         sc=v((2, hf, d, d), BF16), scaled=v((2, hf, d, d), BF16), kpre=v((2, hf, d, d), BF16),
         numer=v((2, hf, d, d), F32), denom=v((2, hf, d, 1), F32), wden=v((2, hf, d, 1), F32),
         kpart=v((2, hf, d, d), F32), vpart=v((2, hf, d, d), F32),
-        own=v((3, 2, hf, d, d), F32), ksown=v((2, 2, g, 8, d), F32),
+        own=v((3, 2, hf, d, d), F32), ksown=v((2, 2, 8, d), F32),
         comb=v((3, g, hc + 1, d, d), F32), recv=v((3, g, n, hc + 1, s.rows, d), F32),
-        back=v((2, g, hc, d, d), F32), kback=v((2, g, 8, d), F32),
+        back=v((2, g, hc, d, d), F32), kback=v((2, 8, d), F32), mo=v((s.heads, d, d), F32),
         tsum=v((g, hc, s.rows, d), F32), zr=v((g, s.nz, s.rows, d), F32), fin=v((g, hc, s.rows, d), F32),
         outs=v((3, 2, d, wide), F32), outr=v((3, d, wide), F32),
-        in_sem=dma((9,)), sws_sem=dma((4,)), swr_sem=dma((4,)), os_sem=dma((3,)), or_sem=dma((3,)),
+        in_sem=dma((9,)), out_sem=dma((2, g)), sws_sem=dma((4, g)), swr_sem=dma((4, g)), met_sem=pltpu.SemaphoreType.REGULAR((2,)), os_sem=dma((3,)), or_sem=dma((3,)),
         as_sem=dma((3, g)), ar_sem=dma((3, g)),
         bs_sem=dma((3, g)), br_sem=dma((2, g)), mr_sem=dma((g, s.ny)),
         ys_sem=dma((g,)), yr_sem=dma((g,)),
@@ -72,8 +72,9 @@
 KEY, VALUE, QUERY, GRAD = range(4)
 
 
-def kernel(s, names, q_hbm, k_hbm, v_hbm, g_hbm, w_hbm, qo, ko, vo, mo, *refs):
+def kernel(s, names, q_hbm, k_hbm, v_hbm, g_hbm, w_hbm, qo, ko, vo, mg_hbm, *refs):
     r = dict(zip(names, refs))
+    mo = r["mo"]
     n, hc, d, half, rows, ny = s.chips, s.hc, s.dim, s.half, s.rows, s.ny
     wide = half * d
     z = lax.axis_index("dp")
@@ -109,11 +110,23 @@
     def greet(device):
         pl.semaphore_signal(barrier, inc=1, device_id=device, device_id_type=pl.DeviceIdType.MESH)
 
-    for to in depths:
+    below, above = wrap(z + s.nz - 1, s.nz), wrap(z + 1, s.nz)
+    near = (below, above) if s.nz > 2 else (above,)
+    for to in near:
         greet((to, ctx))
     for to in peers:
         greet((z, to * 2 + core))
     greet(sibling)
+
+    def meet(turn):
+        turns = s.nz // 2 - 1
+        if 1 < turn <= turns + 1:
+            for i in range(2):
+                pl.semaphore_wait(r["met_sem"].at[i], 1)
+        if turn <= turns:
+            for i, to in enumerate((above, below)):
+                pl.semaphore_signal(
+                    r["met_sem"].at[i], inc=1, device_id=(to, ctx), device_id_type=pl.DeviceIdType.MESH)
 
     inputs = (k_hbm, v_hbm, q_hbm, g_hbm)
     away = [pltpu.make_async_copy(x.at[0, :, half_of(1 - core)], r["xout"].at[a], r["in_sem"].at[a])
@@ -131,14 +144,15 @@
         away[a].wait()
         r["swap"][a] = r["xout"][a].astype(F32)
 
-    def swap_send(a):
+    def swap_send(a, g):
         for part in range(2):
-            at = pl.ds(part * (d // 2), d // 2)
-            remote(r["swap"].at[a, at], r["got"].at[a, at], r["sws_sem"].at[a], r["swr_sem"].at[a], sibling).start()
-
-    def swap_in(a):
-        wait_for(r["got"].at[a], r["swr_sem"].at[a])
-        r["xin"][a, 1 - core] = r["got"][a].astype(BF16)
+            at = (a, pl.ds(part * (d // 2), d // 2), pl.ds(g * hc * d, hc * d))
+            remote(r["swap"].at[at], r["got"].at[at], r["sws_sem"].at[a, g], r["swr_sem"].at[a, g], sibling).start()
+
+    def swap_in(a, g):
+        at = slice(g * hc * d, (g + 1) * hc * d)
+        wait_for(r["got"].at[a, :, at], r["swr_sem"].at[a, g])
+        r["xin"][a, 1 - core, :, at] = r["got"][a, :, at].astype(BF16)
 
     place_t = lax.broadcasted_iota(jnp.int32, (d, d), 0)
     place_s = lax.broadcasted_iota(jnp.int32, (d, d), 1)
@@ -162,17 +176,20 @@
             r["dk"][b, u] = jnp.minimum(k_feat, 1.0)
             yield 1
             r["own"][0, b, u] = tn(kf, block(VALUE, b, u))
-            r["ksown"][0, b, g, i:i + 1, :] = jnp.sum(kf.astype(F32), axis=0, keepdims=True)
+            r["ksown"][0, b, u:u + 1, :] = jnp.sum(kf.astype(F32), axis=0, keepdims=True)
 
         heads_of(g, stage, (b,))
 
+    def tiles_of(phase, g):
+        return hc + 1 if phase < 2 and g == s.groups - 1 else hc
+
     def send_rows(phase, g):
-        tiles = hc + 1 if phase < 2 else hc
+        tiles = tiles_of(phase, g)
         for i in range(hc):
             u = g * hc + i
             r["comb"][phase, g, i] = r["own"][phase, 0, u] + r["own"][phase, 1, u]
-        if phase < 2:
-            total = r["ksown"][phase, 0, g] + r["ksown"][phase, 1, g]
+        if tiles > hc:
+            total = r["ksown"][phase, 0] + r["ksown"][phase, 1]
             r["comb"][phase, g, hc] = jnp.concatenate([total] * (d // 8), axis=0)
         for to in peers:
             remote(r["comb"].at[phase, g, pl.ds(0, tiles), rows_of(to), :],
@@ -181,8 +198,7 @@
         r["recv"][phase, g, chip, 0:tiles] = r["comb"][phase, g, 0:tiles, rows_of(chip), :]
 
     def wait_rows(phase, g, sem):
-        tiles = hc + 1 if phase < 2 else hc
-        wait_for(r["recv"].at[phase, g, pl.ds(0, n - 1), pl.ds(0, tiles)], sem)
+        wait_for(r["recv"].at[phase, g, pl.ds(0, n - 1), pl.ds(0, tiles_of(phase, g))], sem)
 
     def scan(phase, g):
         wait_rows(phase, g, r["ar_sem"].at[phase, g])
@@ -197,11 +213,12 @@
                    r["back"].at[phase, g, :, rows_of(chip), :],
                    r["bs_sem"].at[phase, g], r["br_sem"].at[phase, g], (z, to * 2 + core)).start()
         r["back"][phase, g, :, rows_of(chip), :] = recv[phase, g, chip, 0:hc]
-        ks = jnp.zeros((8, d), F32)
-        for i in range(n):
-            before = (chip > i) if phase == 0 else (chip < i)
-            ks = ks + jnp.where(before, recv[phase, g, i, hc, 0:8, :], 0.0)
-        r["kback"][phase, g] = ks
+        if tiles_of(phase, g) > hc:
+            ks = jnp.zeros((8, d), F32)
+            for i in range(n):
+                before = (chip > i) if phase == 0 else (chip < i)
+                ks = ks + jnp.where(before, recv[phase, g, i, hc, 0:8, :], 0.0)
+            r["kback"][phase] = ks
 
     def returned(phase, g):
         wait_for(r["back"].at[phase, g, :, pl.ds(0, (n - 1) * rows), :], r["br_sem"].at[phase, g])
@@ -213,9 +230,10 @@
         return state.astype(BF16)
 
     def sum_of(phase, b, g, i):
-        total = r["kback"][phase, g, i:i + 1, :]
+        u = g * hc + i
+        total = r["kback"][phase, u:u + 1, :]
         if b != phase:
-            total = total + r["ksown"][phase, phase, g, i:i + 1, :]
+            total = total + r["ksown"][phase, phase, u:u + 1, :]
         return total
 
     def local_scores(g, blocks=(0, 1)):
@@ -253,7 +271,7 @@
             r["wden"][b, u] = wden
             yield 1
             r["own"][1, b, u] = tn(qf, scaled)
-            r["ksown"][1, b, g, i:i + 1, :] = jnp.sum(wden * qff, axis=0, keepdims=True)
+            r["ksown"][1, b, u:u + 1, :] = jnp.sum(wden * qff, axis=0, keepdims=True)
 
         heads_of(g, stage)
 
@@ -351,44 +369,67 @@
             part = mo.at[heads, pl.ds(start, ny * rows), :]
             remote(part, part, r["ys_sem"].at[g], r["yr_sem"].at[g], sibling).start()
 
+    def store(which, g):
+        heads = pl.ds(which * half + g * hc, hc)
+        return pltpu.make_async_copy(mo.at[heads], mg_hbm.at[heads], r["out_sem"].at[0 if which is core else 1, g])
+
     first, last = groups[:-1], s.groups - 1
     swap_out(KEY)
-    pl.semaphore_wait(barrier, n + s.nz - 1)
-    swap_send(KEY)
     swap_out(VALUE)
-    swap_send(VALUE)
     load_w.wait()
     home[KEY].wait()
     home[VALUE].wait()
-    swap_in(KEY)
-    swap_in(VALUE)
-    for g in groups:
-        key_features(g, 0)
-        key_features(g, 1)
+    for g in groups:
+        key_features(g, core)
+    pl.semaphore_wait(barrier, n + len(near))
+    for g in groups:
+        swap_send(KEY, g)
+        swap_send(VALUE, g)
+    turn = 0
+    for g in groups:
+        swap_in(KEY, g)
+        swap_in(VALUE, g)
+        key_features(g, 1 - core)
         send_rows(0, g)
+        turn += 1
+        meet(turn)
     for a in (QUERY, GRAD):
         swap_out(a)
-        swap_send(a)
+        for g in groups:
+            swap_send(a, g)
         home[a].wait()
-    swap_in(QUERY)
+    for g in groups:
+        swap_in(QUERY, g)
     for g in first:
         local_scores(g)
         scan(0, g)
+        turn += 1
+        meet(turn)
     local_scores(last, (0,))
     scan(0, last)
+    turn += 1
+    meet(turn)
     local_scores(last, (1,))
-    swap_in(GRAD)
+    for g in groups:
+        swap_in(GRAD, g)
     for g in groups:
         returned(0, g)
         attend(g)
         send_rows(1, g)
+        turn += 1
+        meet(turn)
     query_side(0)
     for g in first:
         query_side(g + 1, (0,))
         scan(1, g)
+        turn += 1
+        meet(turn)
         query_side(g + 1, (1,))
     scan(1, last)
     give_out(0)
+    while turn < s.nz // 2:
+        turn += 1
+        meet(turn)
     for g in groups:
         returned(1, g)
         key_side(g)
@@ -401,39 +442,54 @@
         sum_chips(g)
     for a in range(3):
         take_out(a)
-    for g in groups:
-        sum_docs(g)
-    for g in groups:
-        spread(g)
-    for g in groups:
-        collect(g)
-    other = (1 - core) * half
-    for g in groups:
-        wait_for(mo.at[pl.ds(other + g * hc, hc)], r["yr_sem"].at[g])
-
     for a in range(4):
-        wait_for(r["got"].at[a], r["sws_sem"].at[a])
+        for g in groups:
+            wait_for(r["got"].at[a, :, pl.ds(g * hc * d, hc * d)], r["sws_sem"].at[a, g])
     for a in range(3):
         wait_for(r["outr"].at[a], r["os_sem"].at[a])
     for g in groups:
         for phase in range(3):
             wait_rows(phase, g, r["as_sem"].at[phase, g])
+        for phase in range(2):
             wait_for(r["recv"].at[phase, g, pl.ds(0, n - 1), pl.ds(0, hc)], r["bs_sem"].at[phase, g])
+    for g in groups:
+        sum_docs(g)
+    for g in groups:
+        spread(g)
+    for g in groups:
+        collect(g)
+        store(core, g).start()
+    other = 1 - core
+    for g in groups:
+        wait_for(mo.at[pl.ds(other * half + g * hc, hc)], r["yr_sem"].at[g])
+        store(other, g).start()
+    for g in groups:
+        wait_for(r["recv"].at[2, g, pl.ds(0, n - 1), pl.ds(0, hc)], r["bs_sem"].at[2, g])
         wait_for(mo.at[pl.ds(0, hc)], r["ys_sem"].at[g])
         wait_for(r["zr"].at[g, pl.ds(0, s.nz - 1)], r["z1s_sem"].at[g])
         if hc > 1:
             wait_for(r["fin"].at[g, pl.ds(0, hc - 1)], r["z2s_sem"].at[g])
-
-
-def write_out(*refs):
-    count = len(refs) // 2
-    sems = refs[-1]
-    copies = []
-    for i, (src, dst) in enumerate(zip(refs[:count], refs[count:-1])):
-        copies.append(pltpu.make_async_copy(src, dst, sems.at[i]))
-    for copy in copies:
+    for g in groups:
+        store(core, g).wait()
+        store(other, g).wait()
+
+
+def write_out(q, k, v, m, qg, kg, vg, mg, sems, held):
+    size = m.shape[0] // 4
+    parts = [pl.ds(part * size, size) for part in range(4)]
+    reads = [pltpu.make_async_copy(m.at[at], held.at[at], sems.at[i]) for i, at in enumerate(parts)]
+    writes = [pltpu.make_async_copy(held.at[at], mg.at[at], sems.at[4 + i]) for i, at in enumerate(parts)]
+    rows = q.shape[1] // 2
+    for src, dst in ((q, qg), (k, kg), (v, vg)):
+        for part in range(2):
+            at = pl.ds(part * rows, rows)
+            writes.append(pltpu.make_async_copy(src.at[0, at], dst.at[0, at], sems.at[4 + len(writes)]))
+    for copy in reads + writes[4:]:
         copy.start()
-    for copy in copies:
+    for read, write in zip(reads, writes):
+        read.wait()
+        write.start()
+    for copy in writes:
         copy.wait()
 
 
@@ -450,7 +506,7 @@
             functools.partial(kernel, s, tuple(spaces)),
             out_shape=shapes,
             in_specs=[pl.BlockSpec(memory_space=pltpu.HBM)] * 5,
-            out_specs=(pl.BlockSpec(memory_space=pltpu.VMEM),) * 4,
+            out_specs=(pl.BlockSpec(memory_space=pltpu.VMEM),) * 3 + (pl.BlockSpec(memory_space=pltpu.HBM),),
             scratch_shapes=list(spaces.values()),
             compiler_params=pltpu.CompilerParams(
                 collective_id=0, has_side_effects=True, vmem_limit_bytes=52 * 1024 * 1024),
@@ -460,10 +516,10 @@
         return pl.pallas_call(
             write_out,
             out_shape=shapes,
-            in_specs=[pl.BlockSpec(memory_space=pltpu.VMEM)] * 4,
+            in_specs=[pl.BlockSpec(memory_space=pltpu.VMEM)] * 3 + [pl.BlockSpec(memory_space=pltpu.HBM)],
             out_specs=(pl.BlockSpec(memory_space=pltpu.HBM),) * 4,
-            scratch_shapes=[pltpu.SemaphoreType.DMA((4,))],
-            compiler_params=pltpu.CompilerParams(vmem_limit_bytes=4 * 1024 * 1024),
+            scratch_shapes=[pltpu.SemaphoreType.DMA((14,)), pltpu.VMEM(map_weight.shape, F32)],
+            compiler_params=pltpu.CompilerParams(vmem_limit_bytes=52 * 1024 * 1024),
         )(*grads)
 
     split = P("dp", "ctx", None)

time: 80.1 us -> 75.8 us (0.946)
  Pallas kernels: 78 us -> 75 us
  local copies, waits for them, and re-layouts: 1.22 us -> 0 us
    pallas_call x1, Pallas kernels: 76.5 us -> 72.4 us  [per_device(): pl.pallas_call(functools.partial(kernel, s, tuple(spaces)), out_shape=sha...]
    unnamed x2 -> x0, local copies, waits for them, and re-layouts: 1.22 us -> none
    pallas_call x1, Pallas kernels: 1.52 us -> 2.59 us  [per_device(): pl.pallas_call(write_out, out_shape=shapes, in_specs=[pl.BlockSpec(memory...]
where the time goes in v3:
time: 75.8 us; the launch traced here: 75.6 us
  Pallas kernels  75 us (99%)
    pallas_call x1, Pallas kernels, per_device(): pl.pallas_call(functools.partial(kernel, s, tuple(spaces)), out_shape=sha...  72.4 us
    pallas_call x1, Pallas kernels, per_device(): pl.pallas_call(write_out, out_shape=shapes, in_specs=[pl.BlockSpec(memory...  2.59 us

profile of v3, /device:TPU:1, one launch (start us, length us, event | category | flops | bytes accessed | tf_op | source)
XLA Modules:
  0.0 75.6 jit_solution(11433351580010407491)
XLA Ops:
  0.6 72.4 %shard_map.84 = (bf16[1,128,2048]{2,1,0:T(8,128)(2,1)S(1)}, bf16[1,128,2048]{2,1,0:T(8,128)(2,1)S(1)}, bf16[1,128,2048]{2,1,0:T(8,128)(2,1)S(1)}, f32[16,128,128]{2,1,0:T(8,128)}) custom-call(bf16[1,128,2048]{2,1,0:T(8,128)(2,1)} %q_hbm.1, bf16[1,128,2048]{2,1,0:T(8,128)(2,1)} %k_hbm.1, bf16[1,128,2048]{2,1,0:T(8,128)(2,1)} %v_hbm.1, ...), custom_call_target="tpu_custom_call" | custom-call | flops 1207959552 | bytes 5242880 | tf_op jit(solution)/shard_map/pallas_call | solution.py:505
  73.1 2.6 %shard_map.85 = (bf16[1,128,2048]{2,1,0:T(8,128)(2,1)}, bf16[1,128,2048]{2,1,0:T(8,128)(2,1)}, bf16[1,128,2048]{2,1,0:T(8,128)(2,1)}, f32[16,128,128]{2,1,0:T(8,128)}) custom-call(bf16[1,128,2048]{2,1,0:T(8,128)(2,1)S(1)} %get-tuple-element.8.q, bf16[1,128,2048]{2,1,0:T(8,128)(2,1)S(1)} %get-tuple-element.9.k, ...), custom_call_target="tpu_custom_call" | custom-call | tf_op jit(solution)/shard_map/pallas_call | solution.py:516

commit v4 on v3

--- a/solution.py
+++ b/solution.py
@@ -88,8 +88,11 @@
     def wrap(a, size):
         return jnp.where(a >= size, a - size, a)
 
-    peers = [wrap(cx + a, ny) * ny + wrap(cy + b, ny) for a, b in s.plane]
-    depths = [wrap(z + a, s.nz) for a in s.along]
+    def turned(a, size):
+        return jnp.where(core == 0, a, (size - a) % size)
+
+    peers = [wrap(cx + turned(a, ny), ny) * ny + wrap(cy + turned(b, ny), ny) for a, b in s.plane]
+    depths = [wrap(z + turned(a, s.nz), s.nz) for a in s.along]
 
     def remote(src, dst, send, recv, device):
         return pltpu.make_async_remote_copy(

time: 75.8 us -> 75.1 us (level)
  no operation moved by 1% of the time
where the time goes in v4:
time: 75.1 us; the launch traced here: 74.9 us
  Pallas kernels  74.3 us (99%)
    pallas_call x1, Pallas kernels, per_device(): pl.pallas_call(functools.partial(kernel, s, tuple(spaces)), out_shape=sha...  71.7 us
    pallas_call x1, Pallas kernels, per_device(): pl.pallas_call(write_out, out_shape=shapes, in_specs=[pl.BlockSpec(memory...  2.59 us

profile of v4, /device:TPU:1, one launch (start us, length us, event | category | flops | bytes accessed | tf_op | source)
XLA Modules:
  0.0 74.9 jit_solution(8963846444569044935)
XLA Ops:
  0.6 71.7 %shard_map.84 = (bf16[1,128,2048]{2,1,0:T(8,128)(2,1)S(1)}, bf16[1,128,2048]{2,1,0:T(8,128)(2,1)S(1)}, bf16[1,128,2048]{2,1,0:T(8,128)(2,1)S(1)}, f32[16,128,128]{2,1,0:T(8,128)}) custom-call(bf16[1,128,2048]{2,1,0:T(8,128)(2,1)} %q_hbm.1, bf16[1,128,2048]{2,1,0:T(8,128)(2,1)} %k_hbm.1, bf16[1,128,2048]{2,1,0:T(8,128)(2,1)} %v_hbm.1, ...), custom_call_target="tpu_custom_call" | custom-call | flops 1207959552 | bytes 5242880 | tf_op jit(solution)/shard_map/pallas_call | solution.py:508
  72.3 2.6 %shard_map.85 = (bf16[1,128,2048]{2,1,0:T(8,128)(2,1)}, bf16[1,128,2048]{2,1,0:T(8,128)(2,1)}, bf16[1,128,2048]{2,1,0:T(8,128)(2,1)}, f32[16,128,128]{2,1,0:T(8,128)}) custom-call(bf16[1,128,2048]{2,1,0:T(8,128)(2,1)S(1)} %get-tuple-element.8.q, bf16[1,128,2048]{2,1,0:T(8,128)(2,1)S(1)} %get-tuple-element.9.k, ...), custom_call_target="tpu_custom_call" | custom-call | tf_op jit(solution)/shard_map/pallas_call | solution.py:519

commit v5 on v4

--- a/solution.py
+++ b/solution.py
@@ -345,7 +345,7 @@
         r["fin"][g, tile] = acc
         for off in range(-(hc // 2), hc - hc // 2):
             if off != 0:
-                to = wrap(z + off % s.nz, s.nz)
+                to = wrap(z + turned(off % s.nz, s.nz), s.nz)
                 remote(r["fin"].at[g, tile], r["fin"].at[g, tile], r["z2s_sem"].at[g],
                        r["z2r_sem"].at[g], (to, ctx)).start()
 

time: 75.1 us -> 75.2 us (level)
  no operation moved by 1% of the time
where the time goes in v5:
time: 75.2 us; the launch traced here: 75 us
  Pallas kernels  74.4 us (99%)
    pallas_call x1, Pallas kernels, per_device(): pl.pallas_call(functools.partial(kernel, s, tuple(spaces)), out_shape=sha...  71.8 us
    pallas_call x1, Pallas kernels, per_device(): pl.pallas_call(write_out, out_shape=shapes, in_specs=[pl.BlockSpec(memory...  2.59 us

profile of v5, /device:TPU:1, one launch (start us, length us, event | category | flops | bytes accessed | tf_op | source)
XLA Modules:
  0.0 75.0 jit_solution(3274108794542063808)
XLA Ops:
  0.6 71.8 %shard_map.84 = (bf16[1,128,2048]{2,1,0:T(8,128)(2,1)S(1)}, bf16[1,128,2048]{2,1,0:T(8,128)(2,1)S(1)}, bf16[1,128,2048]{2,1,0:T(8,128)(2,1)S(1)}, f32[16,128,128]{2,1,0:T(8,128)}) custom-call(bf16[1,128,2048]{2,1,0:T(8,128)(2,1)} %q_hbm.1, bf16[1,128,2048]{2,1,0:T(8,128)(2,1)} %k_hbm.1, bf16[1,128,2048]{2,1,0:T(8,128)(2,1)} %v_hbm.1, ...), custom_call_target="tpu_custom_call" | custom-call | flops 1207959552 | bytes 5242880 | tf_op jit(solution)/shard_map/pallas_call | solution.py:508
  72.4 2.6 %shard_map.85 = (bf16[1,128,2048]{2,1,0:T(8,128)(2,1)}, bf16[1,128,2048]{2,1,0:T(8,128)(2,1)}, bf16[1,128,2048]{2,1,0:T(8,128)(2,1)}, f32[16,128,128]{2,1,0:T(8,128)}) custom-call(bf16[1,128,2048]{2,1,0:T(8,128)(2,1)S(1)} %get-tuple-element.8.q, bf16[1,128,2048]{2,1,0:T(8,128)(2,1)S(1)} %get-tuple-element.9.k, ...), custom_call_target="tpu_custom_call" | custom-call | tf_op jit(solution)/shard_map/pallas_call | solution.py:519
